TPU v7x, 32 devices: a whole 2x2x4 slice. The times are simulated.
32 devices in a mesh: section: 2 (over x), dp: 16 (over z, y, core).
Axes of the slice: x: 2, y: 2, z: 4, core: 2. Of those that a mesh axis runs over, the one named last changes fastest.
Arguments:
- inputs: bfloat16 [2, 16, 512, 768], P(None, 'dp'), may hold values from -6 to 6
- cotangent: bfloat16 [2, 16, 512, 768], P(None, 'dp'), may hold values from -6 to 6
- segments: int32 [2, 16, 512], P(None, 'dp'), may hold values from 0 to 3, never falling along the last dimension, each value on 1 to 256 neighbouring positions
- norm1_gain: bfloat16 [2, 768], P('section'), may hold values from 0.5 to 1.5
- norm1_shift: bfloat16 [2, 768], P('section'), may hold values from -1.75 to 1.75
- w_qkv: bfloat16 [2, 768, 2304], P('section'), may hold values from -0.21875 to 0.21875
- bias_query: bfloat16 [2, 768], P('section'), may hold values from -1.75 to 1.75
- bias_value: bfloat16 [2, 768], P('section'), may hold values from -1.75 to 1.75
- w_out: bfloat16 [2, 768, 768], P('section'), may hold values from -1.75 to 1.75
- bias_out: bfloat16 [2, 768], P('section'), may hold values from -1.75 to 1.75
- norm2_gain: bfloat16 [2, 768], P('section'), may hold values from 0.5 to 1.5
- norm2_shift: bfloat16 [2, 768], P('section'), may hold values from -1.75 to 1.75
- w_up: bfloat16 [2, 768, 3072], P('section'), may hold values from -0.21875 to 0.21875
- bias_up: bfloat16 [2, 3072], P('section'), may hold values from -3 to 3
- w_down: bfloat16 [2, 3072, 768], P('section'), may hold values from -0.109375 to 0.109375
- bias_down: bfloat16 [2, 768], P('section'), may hold values from -1.75 to 1.75
Outputs:
- block_out: bfloat16 [2, 2, 16, 512, 768], P('section', None, 'dp')
- input_grad: float32 [2, 2, 16, 512, 768], P('section', None, 'dp')
- grad_norm1_gain: float32 [2, 768], P('section')
- grad_norm1_shift: float32 [2, 768], P('section')
- grad_w_qkv: float32 [2, 768, 2304], P('section')
- grad_bias_query: float32 [2, 768], P('section')
- grad_bias_value: float32 [2, 768], P('section')
- grad_w_out: float32 [2, 768, 768], P('section')
- grad_bias_out: float32 [2, 768], P('section')
- grad_norm2_gain: float32 [2, 768], P('section')
- grad_norm2_shift: float32 [2, 768], P('section')
- grad_w_up: float32 [2, 768, 3072], P('section')
- grad_bias_up: float32 [2, 3072], P('section')
- grad_w_down: float32 [2, 3072, 768], P('section')
- grad_bias_down: float32 [2, 768], P('section')
Inputs may be any that keep to these rules, and one draw needn't show every extreme that they name: `segments`: in each sequence the segment numbers never fall; positions with equal numbers form one packed text-image pair and attend only to one another; a pair has at most 256 positions.
All inputs are finite; a program needn't handle non-finite values.
Results may differ from a plain program's by a relative error of at most 0.017.
Values may be sent and summed in bfloat16 or wider, within the bound.
A program may use at most 320 MiB of HBM per device.

v0:
```python
import functools
import math

import jax
import jax.numpy as jnp
from jax import lax
from jax.experimental import pallas as pl
from jax.experimental.pallas import tpu as pltpu
from jax.sharding import PartitionSpec as P

HEAD_DIM = 64
GROUP = 6
BF = jnp.bfloat16
F32 = jnp.float32
FAR = float(2**30)
VMEM_LIMIT = 60 * 2**20
ANY = pl.BlockSpec(memory_space=pl.ANY)
VM = pl.BlockSpec(memory_space=pltpu.VMEM)
HBM = pl.BlockSpec(memory_space=pltpu.HBM)


def nn(left, right):
    return lax.dot_general(left, right, (((1,), (0,)), ((), ())), preferred_element_type=F32)


def nt(left, right):
    return lax.dot_general(left, right, (((1,), (1,)), ((), ())), preferred_element_type=F32)


def tn(left, right):
    return lax.dot_general(left, right, (((0,), (0,)), ((), ())), preferred_element_type=F32)


def gelu_pair(u):
    d = 1.0 + (0.3275911 / math.sqrt(2.0)) * jnp.abs(u)
    t = pl.reciprocal(d, approx=True)
    t = t * (2.0 - d * t)
    e = jnp.exp(u * u * -0.5)
    poly = 0.5 * 1.061405429
    for c in (-1.453152027, 1.421413741, -0.284496736, 0.254829592):
        poly = poly * t + 0.5 * c
    tail = poly * t * e
    cdf = jnp.where(u >= 0, 1.0 - tail, tail)
    return u * cdf, cdf + u * (e * (1.0 / math.sqrt(2.0 * math.pi)))


def normed(x):
    centred = x - jnp.mean(x, axis=-1, keepdims=True)
    rstd = lax.rsqrt(jnp.mean(centred * centred, axis=-1, keepdims=True) + 1e-06)
    return centred * rstd, rstd


def norm_back(x, gain, cot):
    xh, rstd = normed(x)
    dy = cot * gain
    m1 = jnp.mean(dy, axis=-1, keepdims=True)
    m2 = jnp.mean(dy * xh, axis=-1, keepdims=True)
    return rstd * (dy - m1 - xh * m2), cot * xh


def half_masks(length):
    lane = lax.broadcasted_iota(jnp.int32, (length, 128), 1)
    low = (lane < HEAD_DIM).astype(F32)
    return low.astype(BF), (1.0 - low).astype(BF)


class Outs:
    def __init__(self, sems):
        self.sems = sems
        self.sites = {}

    def start(self, site, src, dst):
        self.sites.setdefault(site, len(self.sites))
        copy = pltpu.make_async_copy(src, dst, self.sems.at[self.sites[site]])
        copy.start()

    def wait(self, site, src, dst):
        self.sites.setdefault(site, len(self.sites))
        pltpu.make_async_copy(src, dst, self.sems.at[self.sites[site]]).wait()


def relay_kernel(seg_ref, x_hbm, cot_hbm, wqkv_hbm, wout_hbm, wup_hbm, wdn_hbm, g1, b1, bq, bv, bo, g2, b2, bu, bd,
                 out_o, gin_o, n1_o, st_o, mt_o, rl_o, n2_o, ul_o, hid_o, dl_o, ln_o, qkv_o, e_o, li_o, rs_o, gp_o,
                 wqkv, wout, wup, wdn, xs, dls, out2, gs, n1, qkv, vt, e_v, li, mt, rs, n2, gp, hid, ul, acc, u_v, s_v, rl, mlt, st, ds_v,
                 k2t_v, dot_v, ln, qc, kc, sem_i, sem_x, sem_o, sem_l, sem_g, fs, fr, bs, br):
    sec = lax.axis_index("section")
    other = (1 - sec, lax.axis_index("dp"))
    micro, length, feats = xs.shape
    ff = hid.shape[1]
    heads = feats // HEAD_DIM
    half = length // 2
    quarter = length // 4
    chunks = ff // feats

    def remote(src, dst, s_sem, r_sem):
        return pltpu.make_async_remote_copy(
            src_ref=src, dst_ref=dst, send_sem=s_sem, recv_sem=r_sem, device_id=other, device_id_type=pl.DeviceIdType.MESH)

    def part(r, size):
        return pl.ds(r * size if isinstance(r, int) else pl.multiple_of(r * size, size), size)

    def send_out(m, r):
        rows = part(r, half)
        return remote(out2.at[m, rows], xs.at[m, rows], fs.at[m, r], fr.at[m, r])

    def send_grad(m, r):
        rows = part(r, quarter)
        return remote(gs.at[m, rows], dls.at[m, rows], bs.at[m, r], br.at[m, r])

    def load_x(m):
        return pltpu.make_async_copy(x_hbm.at[m, 0], xs.at[m], sem_x.at[m])

    def load_cot(m):
        return pltpu.make_async_copy(cot_hbm.at[m, 0], dls.at[m], sem_x.at[m])

    barrier = pltpu.get_barrier_semaphore()
    pl.semaphore_signal(barrier, inc=1, device_id=other, device_id_type=pl.DeviceIdType.MESH)
    w_qkv, w_out, w_up, w_dn = [
        pltpu.make_async_copy(src.at[0], dst, sem_i.at[i])
        for i, (src, dst) in enumerate(((wqkv_hbm, wqkv), (wout_hbm, wout), (wup_hbm, wup), (wdn_hbm, wdn)))]

    @pl.when(sec == 0)
    def _():
        load_x(0).start()

    for c in (w_qkv, w_out, w_up, w_dn):
        c.start()

    @pl.when(sec == 0)
    def _():
        for m in range(1, micro):
            load_x(m).start()

    @pl.when(sec != 0)
    def _():
        for m in range(micro):
            load_cot(m).start()

    pl.semaphore_wait(barrier, 1)
    outs = Outs(sem_o)
    lows = half_masks(length)
    row_low = (lax.broadcasted_iota(jnp.int32, (128, length), 0) < HEAD_DIM).astype(F32)
    row_lows = (row_low.astype(BF), (1.0 - row_low).astype(BF))

    @pl.loop(0, micro)
    def _(m):
        def before(*sites):
            @pl.when(m > 0)
            def _():
                for site, src, dst in sites:
                    outs.wait(site, src, dst)

        seg = jnp.broadcast_to(seg_ref[m], (128, length))
        row = lax.broadcasted_iota(jnp.int32, (128, length), 0) % HEAD_DIM
        kcode = (seg == row).astype(F32)
        qcode = jnp.where(row < 4, -FAR * (1.0 - kcode), 0.0)
        kc[...] = kcode.T.astype(BF)
        qc[...] = qcode.T.astype(BF)

        @pl.when(sec == 0)
        def _():
            load_x(m).wait()

        before(("n1", n1, n1_o.at[0]), ("qkv", qkv, qkv_o))
        @pl.loop(0, 2)
        def _(r):
            @pl.when(sec != 0)
            def _():
                send_out(m, r).wait_recv()

            @pl.loop(0, half // 128)
            def _(i):
                rows = pl.ds(pl.multiple_of(r * half + i * 128, 128), 128)
                xh, _ = normed(xs[m, rows, :].astype(F32))
                n1[rows, :] = (xh * g1[...].astype(F32) + b1[...].astype(F32)).astype(BF)

            @pl.when(jnp.logical_and(m == 0, r == 0))
            def _():
                w_qkv.wait()

            rows = part(r, half)
            q = (nn(n1[rows, :], wqkv[:, :feats]) + bq[...].astype(F32)) * HEAD_DIM ** -0.5
            qkv[rows, :feats] = q.astype(BF)
            qkv[rows, feats:2 * feats] = nn(n1[rows, :], wqkv[:, feats:2 * feats]).astype(BF)
            v = nn(n1[rows, :], wqkv[:, 2 * feats:]) + bv[...].astype(F32)
            qkv[rows, 2 * feats:] = v.astype(BF)
            vt[:, rows] = v.T.astype(BF)

        outs.start("n1", n1, n1_o.at[m])
        before(("e", e_v, e_o), ("li", li, li_o), ("mt", mt, mt_o.at[0]))

        @pl.loop(0, heads // GROUP)
        def _(group):
            def spot(i):
                return group * GROUP + i, pl.multiple_of((group * (GROUP // 2) + i // 2) * 128, 128), i % 2

            def score(i):
                _, at, h = spot(i)
                qa = qkv[:, pl.ds(at, 128)] * lows[h] + qc[...] * lows[1 - h]
                ka = qkv[:, pl.ds(feats + at, 128)] * lows[h] + kc[...] * lows[1 - h]
                s_v[i % 2] = nt(ka, qa)

            def expo(i):
                scores = s_v[i % 2]
                e_v[spot(i)[0]] = jnp.exp(scores - jnp.max(scores, axis=0, keepdims=True)).astype(BF)

            def mix(i):
                head, at, h = spot(i)
                ot = nn(vt[pl.ds(at, 128), :] * row_lows[h] + row_lows[1 - h], e_v[head])
                mine, ones = (slice(0, 64), slice(64, 65)) if h == 0 else (slice(64, 128), slice(0, 1))
                inv = 1.0 / ot[ones]
                li[pl.ds(head, 1), :] = inv
                mt[pl.ds(pl.multiple_of(head * HEAD_DIM, HEAD_DIM), HEAD_DIM), :] = (ot[mine] * inv).astype(BF)

            for t in range(GROUP + 2):
                if t < GROUP:
                    score(t)
                if 0 <= t - 2:
                    mix(t - 2)
                if 0 <= t - 1 < GROUP:
                    expo(t - 1)

        outs.start("mt", mt, mt_o.at[m])
        before(("rs", rs, rs_o), ("n2", n2, n2_o.at[0]))

        @pl.when(m == 0)
        def _():
            w_out.wait()

        rs[...] = xs[m].astype(F32) + tn(mt[...], wout[...]) + bo[...].astype(F32)

        @pl.loop(0, length // 128)
        def _(i):
            rows = pl.ds(pl.multiple_of(i * 128, 128), 128)
            xh, _ = normed(rs[rows, :])
            n2[rows, :] = (xh * g2[...].astype(F32) + b2[...].astype(F32)).astype(BF)

        outs.start("n2", n2, n2_o.at[m])
        before(("gp", gp, gp_o), ("hid", hid, hid_o.at[0]))

        @pl.when(m == 0)
        def _():
            w_up.wait()
            w_dn.wait()
            outs.start("qkv", qkv, qkv_o)
            outs.start("e", e_v, e_o)
            outs.start("li", li, li_o)
            outs.start("rs", rs, rs_o)

        tiles = [(r, j) for r in range(2) for j in range(chunks)]

        def place(t):
            r, j = tiles[t]
            return slice(r * half, (r + 1) * half), slice(j * feats, (j + 1) * feats)

        def up(t):
            rows, cols = place(t)
            u_v[t % 2] = nn(n2[rows, :], wup[:, cols])

        def act(t):
            rows, cols = place(t)
            h, g = gelu_pair(u_v[t % 2] + bu[:, cols].astype(F32))
            hid[rows, cols] = h.astype(BF)
            gp[rows, cols] = g.astype(BF)

        def down(t):
            rows, cols = place(t)
            term = nn(hid[rows, cols], wdn[cols, :])
            r, j = tiles[t]
            if j == 0:
                acc[rows, :] = rs[rows, :] + bd[...].astype(F32) + term
            elif j < chunks - 1:
                acc[rows, :] = acc[rows, :] + term
            else:
                out2[m, rows, :] = (acc[rows, :] + term).astype(BF)

                @pl.when(sec == 0)
                def _():
                    send_out(m, r).start()

        for t in range(len(tiles) + 2):
            if t < len(tiles):
                up(t)
            if 0 <= t - 2:
                down(t - 2)
            if 0 <= t - 1 < len(tiles):
                act(t - 1)

        before(("out", out2.at[0], out_o.at[0]))
        outs.start("out", out2.at[m], out_o.at[m])
        outs.start("hid", hid, hid_o.at[m])

        @pl.when(m == 0)
        def _():
            outs.start("gp", gp, gp_o)

    lane = lax.broadcasted_iota(jnp.int32, (length, 128), 1)
    ones = ((jnp.logical_and(lane >= 64, lane < 66)).astype(F32).astype(BF), (lane < 2).astype(F32).astype(BF))
    low_f = lane < HEAD_DIM
    fill = jnp.zeros((62, length), BF)

    def gin_copy(m, r):
        return pltpu.make_async_copy(rs.at[part(r, quarter)], gin_o.at[m, part(r, quarter)], sem_g.at[r])
    @pl.loop(0, micro)
    def _(step):
        m = micro - 1 - step

        def before(*sites):
            @pl.when(step > 0)
            def _():
                for site, src, dst in sites:
                    outs.wait(site, src, dst)

        loads = [pltpu.make_async_copy(a, b, sem_l.at[i]) for i, (a, b) in enumerate(
            ((gp_o, gp), (rs_o, rs), (mt_o.at[0], mt), (li_o, li), (qkv_o, qkv), (e_o, e_v)))]
        l_gp, l_rs, l_mt, l_li, l_qkv, l_e = loads

        def loaded(*copies):
            @pl.when(step > 0)
            def _():
                for c in copies:
                    c.wait()

        def fetch(*copies):
            @pl.when(step == 0)
            def _():
                for c in copies:
                    c.start()

        @pl.when(sec != 0)
        def _():
            load_cot(m).wait()

        loaded(l_gp)
        before(("ul", ul, ul_o.at[0]))
        @pl.loop(0, 2)
        def _(r):
            @pl.when(sec == 0)
            def _():
                send_grad(m, 2 * r).wait_recv()
                send_grad(m, 2 * r + 1).wait_recv()

            rows = part(r, half)
            for j in range(chunks):
                cols = slice(j * feats, (j + 1) * feats)
                ul[rows, cols] = (nt(dls[m, rows, :], wdn[cols, :]) * gp[rows, cols].astype(F32)).astype(BF)
        fetch(l_gp)

        @pl.when(step > 0)
        def _():
            for r in range(4):
                gin_copy(0, r).wait()
            l_rs.start()

        acc[...] = nt(ul[...], wup[...])
        before(("dl", dls.at[0], dl_o.at[0]), ("rl", rl, rl_o.at[0]), ("ln", ln, ln_o.at[0]))
        outs.start("dl", dls.at[m], dl_o.at[m])
        outs.start("ul", ul, ul_o.at[m])
        loaded(l_rs)
        ln[...] = jnp.zeros_like(ln)

        @pl.loop(0, length // 128)
        def _(i):
            rows = pl.ds(pl.multiple_of(i * 128, 128), 128)
            cot = acc[rows, :]
            dx, gx = norm_back(rs[rows, :], g2[...].astype(F32), cot)
            ln[2:3, :] += jnp.sum(gx, axis=0, keepdims=True)
            ln[3:4, :] += jnp.sum(cot, axis=0, keepdims=True)
            res = dls[m, rows, :].astype(F32) + dx
            rs[rows, :] = res
            rl[rows, :] = res.astype(BF)

        outs.start("rl", rl, rl_o.at[m])
        mlt[...] = nt(wout[...], rl[...]).astype(BF)
        loaded(l_mt, l_li, l_qkv, l_e)
        before(("st", st, st_o.at[0]))

        @pl.loop(0, heads // GROUP)
        def _(group):
            keep = {}

            def spot(i):
                return group * GROUP + i, pl.multiple_of((group * (GROUP // 2) + i // 2) * 128, 128), i // 2 % 2, i % 2

            def probe(i):
                head, at, p, h = spot(i)
                if h == 0:
                    k2t_v[p] = qkv[:, pl.ds(feats + at, 128)].astype(F32).T.astype(BF)
                    scale = jnp.concatenate([jnp.broadcast_to(li[pl.ds(head + g, 1), :], (64, length)) for g in (0, 1)], axis=0)
                    dot_v[p] = (mlt[pl.ds(at, 128), :].astype(F32) * scale).astype(BF)
                mine = dot_v[p, 64 * h:64 * h + 64, :]
                mixed = mt[pl.ds(pl.multiple_of(head * HEAD_DIM, HEAD_DIM), HEAD_DIM), :]
                delta = -jnp.sum(mine.astype(F32) * mixed.astype(F32), axis=0, keepdims=True)
                d_hi = delta.astype(BF)
                d_lo = (delta - d_hi.astype(F32)).astype(BF)
                extra = jnp.concatenate([d_hi, d_lo, fill], axis=0)
                da = jnp.concatenate((mine, extra) if h == 0 else (extra, mine), axis=0)
                va = qkv[:, pl.ds(2 * feats + at, 128)] * lows[h] + ones[h]
                s_v[i % 2] = nn(va, da)

            def scale_back(i):
                ds_v[i % 2] = (e_v[spot(i)[0]].astype(F32) * s_v[i % 2]).astype(BF)

            def spread(i):
                head, at, p, h = spot(i)
                ds = ds_v[i % 2]
                dv = nt(e_v[head], dot_v[p])
                dk = nn(ds, qkv[:, pl.ds(at, 128)])
                dq = nn(k2t_v[p], ds)[64 * h:64 * h + 64]
                if h == 0:
                    keep[p] = (dv, dk, dq)
                    return
                first = keep.pop(p)
                st[:, pl.ds(2 * feats + at, 128)] = jnp.where(low_f, first[0], dv).astype(BF)
                st[:, pl.ds(feats + at, 128)] = jnp.where(low_f, first[1], dk).astype(BF)
                q = jnp.concatenate([first[2], dq], axis=0).astype(BF).astype(F32) * HEAD_DIM ** -0.5
                st[:, pl.ds(at, 128)] = q.T.astype(BF)

            for t in range(GROUP + 1):
                if t < GROUP:
                    probe(t)
                if 0 <= t - 1:
                    scale_back(t - 1)
                    spread(t - 1)

        outs.start("st", st, st_o.at[m])

        @pl.when(step == 0)
        def _():
            outs.wait("mt", mt, mt_o.at[0])

        fetch(l_mt, l_li, l_qkv, l_e)
        @pl.loop(0, 4)
        def _(r):
            rows = part(r, quarter)
            cot = nt(st[rows, :], wqkv[...])
            dx, gx = norm_back(xs[m, rows, :].astype(F32), g1[...].astype(F32), cot)
            ln[0:1, :] += jnp.sum(gx, axis=0, keepdims=True)
            ln[1:2, :] += jnp.sum(cot, axis=0, keepdims=True)
            res = rs[rows, :] + dx
            rs[rows, :] = res
            gs[m, rows, :] = res.astype(BF)

            @pl.when(sec != 0)
            def _():
                send_grad(m, r).start()

            gin_copy(m, r).start()


        outs.start("ln", ln, ln_o.at[m])

    for site, src, dst in (("dl", dls.at[0], dl_o.at[0]), ("rl", rl, rl_o.at[0]), ("ln", ln, ln_o.at[0]), ("st", st, st_o.at[0]),
                           ("ul", ul, ul_o.at[0]), ("n1", n1, n1_o.at[0]), ("n2", n2, n2_o.at[0]),
                           ("hid", hid, hid_o.at[0]), ("out", out2.at[0], out_o.at[0])):
        outs.wait(site, src, dst)
    for r in range(4):
        gin_copy(0, r).wait()

    @pl.when(sec == 0)
    def _():
        for m in range(micro):
            for r in range(2):
                send_out(m, r).wait_send()

    @pl.when(sec != 0)
    def _():
        for m in range(micro):
            for r in range(4):
                send_grad(m, r).wait_send()


def relay(seg, x, cot, weights, vecs):
    micro, _, length, feats = x.shape
    ff = weights[2].shape[2]
    heads = feats // HEAD_DIM
    sds = jax.ShapeDtypeStruct

    def vmem(dtype, *shape):
        return pltpu.VMEM(shape, dtype)

    outs = [
        sds((micro, length, feats), BF),
        sds((micro, length, feats), F32),
        sds((micro, length, feats), BF),
        sds((micro, length, 3 * feats), BF),
        sds((micro, feats, length), BF),
        sds((micro, length, feats), BF),
        sds((micro, length, feats), BF),
        sds((micro, length, ff), BF),
        sds((micro, length, ff), BF),
        sds((micro, length, feats), BF),
        sds((micro, 8, feats), F32),
        sds((length, 3 * feats), BF),
        sds((heads, length, length), BF),
        sds((16, length), F32),
        sds((length, feats), F32),
        sds((length, ff), BF),
    ]
    dma = pltpu.SemaphoreType.DMA
    return pl.pallas_call(
        relay_kernel,
        out_shape=outs,
        in_specs=[VM] + [ANY] * 6 + [VM] * 9,
        out_specs=[ANY] * len(outs),
        scratch_shapes=[
            vmem(BF, feats, 3 * feats), vmem(BF, feats, feats), vmem(BF, feats, ff), vmem(BF, ff, feats),
            vmem(BF, micro, length, feats), vmem(BF, micro, length, feats), vmem(BF, micro, length, feats), vmem(BF, micro, length, feats),
            vmem(BF, length, feats), vmem(BF, length, 3 * feats), vmem(BF, feats, length), vmem(BF, heads, length, length),
            vmem(F32, 16, length), vmem(BF, feats, length), vmem(F32, length, feats), vmem(BF, length, feats),
            vmem(BF, length, ff), vmem(BF, length, ff), vmem(BF, length, ff), vmem(F32, length, feats), vmem(F32, 2, length // 2, feats),
            vmem(F32, 2, length, length), vmem(BF, length, feats), vmem(BF, feats, length), vmem(BF, length, 3 * feats),
            vmem(BF, 2, length, length), vmem(BF, 2, 128, length), vmem(BF, 2, 128, length), vmem(F32, 8, feats),
            vmem(BF, length, 128), vmem(BF, length, 128),
            dma((4,)), dma((micro,)), dma((16,)), dma((6,)), dma((4,)),
            dma((micro, 2)), dma((micro, 2)), dma((micro, 4)), dma((micro, 4)),
        ],
        compiler_params=pltpu.CompilerParams(vmem_limit_bytes=VMEM_LIMIT, collective_id=1, has_side_effects=True),
        name="layer_relay",
    )(seg, x, cot, *weights, *vecs)


INNER = 16
MASKS = (1, 2, 4, 8)
LAG = dict(s1=1, s2=3, line1=4, line2=2, end2=7, ag1=7, age=7, agy2=9, core=12, done=14)


def exchange_kernel(group, n1_hbm, st_hbm, mt_hbm, rl_hbm, n2_hbm, ul_hbm, hid_hbm, dl_hbm, ln_ref, g_o, small_o, xb,
                    a_v, b_v, mt_v, own, sb0, rb0, sby, rby, line1, line2, sbe, rbe, gath, xv, small, rsm, xsm,
                    ld_sem, out_sem, cs, cr, ys, yr, ls, lr, es, er, as_, ar, ms, mr, xs, xr, xl):
    sec = lax.axis_index("section")
    me = lax.axis_index("dp")
    size = gath.shape[1]
    half, wide, q4, q8 = size // 2, size // 2, size // 4, size // 8
    outer = group // INNER
    kq, ku, kd = st_hbm.shape[2] // size, ul_hbm.shape[2] // size, hid_hbm.shape[2] // size
    kinds = (("down", 0, kd), ("up", kd, kd + ku), ("out", kd + ku, kd + ku + 1), ("qkv", kd + ku + 1, kd + ku + 1 + kq))
    count = kinds[-1][2]
    core, y, z = me % 2, (me // 2) % 2, (me // 4) % 4
    left, right = slice(0, wide), slice(wide, size)

    def to(device):
        return dict(device_id=(sec, device), device_id_type=pl.DeviceIdType.MESH)

    def peer(mask):
        return me + mask - 2 * mask * ((me // mask) % 2)

    def outer_peer(k):
        return (me + k * INNER) % group

    barrier = pltpu.get_barrier_semaphore()
    at_end = jnp.logical_or(z == 0, z == 3)
    for mask in MASKS:
        pl.semaphore_signal(barrier, inc=1, **to(peer(mask)))
    for k in range(1, outer):
        pl.semaphore_signal(barrier, inc=1, **to(outer_peer(k)))

    pl.semaphore_signal(barrier, inc=1, **to(me + 12 - 8 * z))

    def remote(src, dst, s_sem, r_sem, device):
        return pltpu.make_async_remote_copy(src_ref=src, dst_ref=dst, send_sem=s_sem, recv_sem=r_sem, **to(device))

    def rows_of(first, rows):
        return pl.ds(pl.multiple_of(first, 16), rows)

    def by_kind(u, fn):
        for kind, low, high in kinds:
            @pl.when(jnp.logical_and(u >= low, u < high))
            def _():
                fn(kind, u - low)

    def block(ref, j, axis):
        cols = pl.ds(pl.multiple_of(j * size, size), size)
        return ref.at[:, :, cols] if axis == 2 else ref.at[:, cols] if axis == 1 else ref.at[cols, :]

    def loads(u):
        def pair(kind, j, act):
            slot = u % 2
            src_a, src_b = {
                "down": lambda: (block(hid_hbm, j, 2), dl_hbm),
                "up": lambda: (n2_hbm, block(ul_hbm, j, 2)),
                "out": lambda: (mt_hbm, rl_hbm),
                "qkv": lambda: (n1_hbm, block(st_hbm, j, 2)),
            }[kind]()
            dst_a = mt_v if kind == "out" else a_v.at[slot]
            act(pltpu.make_async_copy(src_a, dst_a, ld_sem.at[slot, 0]))
            act(pltpu.make_async_copy(src_b, b_v.at[slot], ld_sem.at[slot, 1]))
        return pair

    def start_loads(u):
        by_kind(u, lambda kind, j: loads(u)(kind, j, lambda c: c.start()))

    def core_copy(u):
        return remote(sb0.at[u % 2], rb0.at[u], cs.at[u], cr.at[u], peer(1))

    def y_copy(u):
        return remote(sby.at[u], rby.at[u], ys.at[u], yr.at[u], peer(2))

    def end_copy(u):
        return remote(sbe.at[u], rbe.at[u], es.at[u], er.at[u], peer(2))

    def line_copy(u, part, up):
        ref = line1 if part == 0 else line2
        at = (u, int(up))
        sem = (u, 2 * part + int(up))
        return remote(ref.at[at], ref.at[at], ls.at[sem], lr.at[sem], me + 4 if up else me - 4)

    def compute(u):
        slot = u % 2
        by_kind(u, lambda kind, j: loads(u)(kind, j, lambda c: c.wait()))
        start_loads(u + 1)

        def column():
            return jnp.sum(jnp.sum(b_v[slot].astype(F32), axis=0), axis=0, keepdims=True)

        def products(transposed):
            def product(which):
                cols = pl.ds(pl.multiple_of(which * half, half), half)
                if transposed:
                    total = None
                    for k in range(mt_v.shape[0]):
                        term = nn(mt_v[k, cols, :], b_v[slot, k])
                        total = term if total is None else total + term
                    return total
                value = a_v[slot, :, :, cols]
                tokens = value.shape[0] * value.shape[1]
                return tn(value.reshape(tokens, half), b_v[slot].reshape(tokens, size))

            sb0[slot] = product(1 - core).astype(BF)
            core_copy(u).start()
            own[u % own.shape[0]] = product(core)

        low, high = kinds[2][1], kinds[2][2]
        is_out = jnp.logical_and(u >= low, u < high)

        @pl.when(is_out)
        def _():
            products(True)
            small[5:6, :] = column()

        @pl.when(jnp.logical_not(is_out))
        def _():
            products(False)

        @pl.when(u == 0)
        def _():
            small[4:5, :] = column()

        for j in range(ku):
            @pl.when(u == kinds[1][1] + j)
            def _():
                small[8 + j:9 + j, :] = column()

        for j, at in ((0, 6), (kq - 1, 7)):
            @pl.when(u == kinds[3][1] + j)
            def _():
                small[at:at + 1, :] = column()

    def add_core(u):
        core_copy(u).wait()
        ref = own.at[u % own.shape[0]]
        ref[...] = ref[...] + rb0[u].astype(F32)
        sby[u] = ref[rows_of((1 - y) * q4, q4), left].astype(BF)
        y_copy(u).start()

    def add_y(u):
        y_copy(u).wait()
        ref = own.at[u % own.shape[0]]
        rows = rows_of(y * q4, q4)
        ref[rows, left] = ref[rows, left] + rby[u].astype(F32)

    def along(u, part, up):
        buf = line1 if part == 0 else line2
        ref = own.at[u % own.shape[0]]
        place = z if up else 3 - z
        if part == 0:
            rows, cols = rows_of(y * q4 + (q8 if up else 0), q8), left
        else:
            rows, cols = rows_of(q4 if up else 0, q4), right

        @pl.when(place == 0)
        def _():
            buf[u, int(up)] = ref[rows, cols].astype(BF)

        @pl.when(place > 0)
        def _():
            line_copy(u, part, up).wait_recv()
            total = ref[rows, cols] + buf[u, int(up)].astype(F32)
            ref[rows, cols] = total

            @pl.when(place < 3)
            def _():
                buf[u, int(up)] = total.astype(BF)

        @pl.when(place < 3)
        def _():
            line_copy(u, part, up).start()

        @pl.when(place == 3)
        def _():
            if part == 0:
                rows_up = rows_of(core * half + y * q4 + (q8 if up else 0), q8)
                gath[u, rows_up, left] = over_outer(u, 0, ref[rows, cols]).astype(BF)
            else:
                first = q4 if up else 0
                sbe[u] = ref[rows_of(first + (1 - y) * q8, q8), right].astype(BF)
                end_copy(u).start()

    def over_outer(u, part, total):
        if outer == 1:
            return total
        at = 2 * u + part
        xv[0] = total.astype(BF)
        own_slot = pltpu.make_async_copy(xv.at[0], xb.at[at, 0], xl.at[0])
        own_slot.start()
        copies = [remote(xv.at[0], xb.at[at, k], xs.at[at, k], xr.at[at, k], outer_peer(k)) for k in range(1, outer)]
        for c in copies:
            c.start()
        own_slot.wait()
        for c in copies:
            c.wait()
        back = pltpu.make_async_copy(xb.at[at], xv, xl.at[1])
        back.start()
        back.wait()
        result = None
        for k in range(outer):
            term = xv[(me // INNER - k + outer) % outer].astype(F32)
            result = term if result is None else result + term
        return result

    def part_of(u, part, up):
        if part == 0:
            return gath.at[u, rows_of(core * half + y * q4 + (q8 if up else 0), q8), left]
        return gath.at[u, rows_of(core * half + (q4 if up else 0), q4), right]

    def gather_line(u, part, up):
        ref = part_of(u, part, up)
        sem = (u, 2 * part + int(up))
        return remote(ref, ref, as_.at[sem], ar.at[sem], me - 4 if up else me + 4)

    def gather_y(u, up):
        ref = part_of(u, 0, up)
        sem = (u, 4 + int(up))
        return remote(ref, ref, as_.at[sem], ar.at[sem], peer(2))

    def gather_end(u):
        ref = gath.at[u, rows_of(core * half + (z // 3) * q4 + y * q8, q8), right]
        sem = (u, 6)
        return remote(ref, ref, as_.at[sem], ar.at[sem], peer(2))

    def gather_core(u):
        ref = gath.at[u, rows_of(core * half, half), :]
        sem = (u, 7)
        return remote(ref, ref, as_.at[sem], ar.at[sem], peer(1))

    def finish_end(u):
        @pl.when(at_end)
        def _():
            end_copy(u).wait()
            ref = own.at[u % own.shape[0]]
            total = ref[rows_of((z // 3) * q4 + y * q8, q8), right] + rbe[u].astype(F32)
            gath[u, rows_of(core * half + (z // 3) * q4 + y * q8, q8), right] = over_outer(u, 1, total).astype(BF)

    def end_sent(u):
        @pl.when(at_end)
        def _():
            gather_end(u).start()

    def ends_joined(u):
        @pl.when(at_end)
        def _():
            gather_end(u).wait()

    def back_along(u, part, up):
        place = 3 - z if up else z

        @pl.when(place > 0)
        def _():
            gather_line(u, part, up).wait_recv()

        @pl.when(place < 3)
        def _():
            gather_line(u, part, up).start()

        if part == 0:
            gather_y(u, up).start()

    def to_core(u):
        gather_y(u, False).wait()
        gather_y(u, True).wait()
        gather_core(u).start()

    def out_copy(u):
        return pltpu.make_async_copy(gath.at[u], g_o.at[u], out_sem.at[u])

    def done(u):
        gather_core(u).wait()
        out_copy(u).start()

    def small_copy(stage):
        return remote(small, rsm.at[stage], ms.at[stage], mr.at[stage], peer(MASKS[stage]))

    def small_step(stage):
        small_copy(stage).wait()
        small[...] = small[...] + rsm[stage]
        if stage < 3:
            small_copy(stage + 1).start()
            return
        if outer > 1:
            xsm[0] = small[...]
            copies = [remote(xsm.at[0], xsm.at[k], xs.at[2 * count, k], xr.at[2 * count, k], outer_peer(k)) for k in range(1, outer)]
            for c in copies:
                c.start()
            for c in copies:
                c.wait()
            total = None
            for k in range(outer):
                term = xsm[(me // INNER - k + outer) % outer]
                total = term if total is None else total + term
            small[...] = total
        small_o[...] = small[...]

    start_loads(0)
    small[...] = jnp.zeros_like(small)
    small[0:4, :] = jnp.sum(ln_ref[...], axis=0)[0:4, :]
    pl.semaphore_wait(barrier, len(MASKS) + outer)

    @pl.loop(0, count + LAG["done"])
    def _(tau):
        def at(lag, fn):
            u = tau - lag

            @pl.when(jnp.logical_and(u >= 0, u < count))
            def _():
                fn(u)

        at(LAG["done"], done)
        at(LAG["agy2"], ends_joined)
        at(LAG["s1"], add_core)
        for up in (True, False):
            place = z if up else 3 - z
            at(LAG["line2"] + place, lambda u: along(u, 1, up))
            at(LAG["agy2"] + 3 - place, lambda u: back_along(u, 1, up))
        at(LAG["s2"], add_y)
        for up in (True, False):
            place = z if up else 3 - z
            at(LAG["line1"] + place, lambda u: along(u, 0, up))
        at(LAG["end2"], finish_end)
        at(LAG["age"], end_sent)
        for up in (True, False):
            place = z if up else 3 - z
            at(LAG["ag1"] + 3 - place, lambda u: back_along(u, 0, up))
        at(LAG["core"], to_core)
        at(0, compute)

        @pl.when(tau == count)
        def _():
            small_copy(0).start()

        for stage in range(4):
            @pl.when(tau == count + 2 + 2 * stage)
            def _():
                small_step(stage)

    @pl.loop(0, count)
    def _(u):
        out_copy(u).wait()
        for up in (True, False):
            place = z if up else 3 - z

            @pl.when(place < 3)
            def _():
                for part in (0, 1):
                    line_copy(u, part, up).wait_send()

            @pl.when(place > 0)
            def _():
                for part in (0, 1):
                    gather_line(u, part, up).wait_send()


def exchange(group, n1, st, mt, rl, n2, ul, hid, dl, ln):
    micro, length, feats = n1.shape
    ff = ul.shape[2]
    outer = group // INNER
    count = st.shape[2] // feats + 2 * (ff // feats) + 1
    half, q4, q8 = feats // 2, feats // 4, feats // 8
    sds = jax.ShapeDtypeStruct

    def vmem(dtype, *shape):
        return pltpu.VMEM(shape, dtype)

    dma = pltpu.SemaphoreType.DMA
    return pl.pallas_call(
        functools.partial(exchange_kernel, group),
        out_shape=[sds((count, feats, feats), BF), sds((16, feats), F32),
                   sds((2 * count, outer, q8, half) if outer > 1 else (16, 128), BF)],
        in_specs=[ANY] * 8 + [VM],
        out_specs=[ANY, VM, ANY],
        scratch_shapes=[
            vmem(BF, 2, micro, length, feats),
            vmem(BF, 2, micro, length, feats),
            vmem(BF, micro, feats, length),
            vmem(F32, 8, half, feats),
            vmem(BF, 2, half, feats),
            vmem(BF, count, half, feats),
            vmem(BF, count, q4, half),
            vmem(BF, count, q4, half),
            vmem(BF, count, 2, q8, half),
            vmem(BF, count, 2, q4, half),
            vmem(BF, count, q8, half),
            vmem(BF, count, q8, half),
            vmem(BF, count, feats, feats),
            vmem(BF, outer, q8, half),
            vmem(F32, 16, feats),
            vmem(F32, 4, 16, feats),
            vmem(F32, outer, 16, feats),
            dma((2, 2)),
            dma((count,)),
            dma((count,)), dma((count,)),
            dma((count,)), dma((count,)),
            dma((count, 4)), dma((count, 4)),
            dma((count,)), dma((count,)),
            dma((count, 8)), dma((count, 8)),
            dma((4,)), dma((4,)),
            dma((2 * count + 1, outer)), dma((2 * count + 1, outer)),
            dma((2,)),
        ],
        compiler_params=pltpu.CompilerParams(vmem_limit_bytes=VMEM_LIMIT, collective_id=0, has_side_effects=True),
        name="grad_exchange",
    )(n1, st, mt, rl, n2, ul, hid, dl, ln)[:2]


def finish_kernel(g, small_hbm, block_hbm, gin_hbm, block_o, gin_o, g1_o, s1_o, gq_o, bq_o, bv_o, go_o, bo_o, g2_o, s2_o, gu_o, bu_o, gd_o, bd_o,
                  narrow, stage, small, block, gin, sem_g, sem, sem_b):
    size = g.shape[1]
    loads = [pltpu.make_async_copy(g.at[u], narrow.at[u], sem_g.at[u]) for u in range(g.shape[0])]
    for c in loads:
        c.start()
    load_small = pltpu.make_async_copy(small_hbm, small, sem_b.at[4])
    passing = [pltpu.make_async_copy(block_hbm, block, sem_b.at[0]), pltpu.make_async_copy(gin_hbm, gin, sem_b.at[1])]
    copies = [pltpu.make_async_copy(block, block_o.at[0, :, 0], sem_b.at[2]), pltpu.make_async_copy(gin, gin_o.at[0, :, 0], sem_b.at[3])]
    for c in passing + [load_small]:
        c.start()
    places = [gd_o.at[0, pl.ds(j * size, size), :] for j in range(gd_o.shape[1] // size)]
    for ref in (gu_o, go_o, gq_o):
        places += [ref.at[0, :, pl.ds(j * size, size)] for j in range(ref.shape[2] // size)]
    slots = stage.shape[0]
    running = []
    for u, place in enumerate(places):
        if u >= slots:
            running[u - slots].wait()
        loads[u].wait()
        stage[u % slots] = narrow[u].astype(F32)
        c = pltpu.make_async_copy(stage.at[u % slots], place, sem.at[u])
        c.start()
        running.append(c)
        if u == slots - 1:
            for load, store in zip(passing, copies):
                load.wait()
                store.start()
    load_small.wait()
    for ref, at in ((g1_o, 0), (s1_o, 1), (g2_o, 2), (s2_o, 3), (bd_o, 4), (bo_o, 5), (bq_o, 6), (bv_o, 7)):
        ref[...] = small[at:at + 1, :]
    for j in range(bu_o.shape[1] // size):
        bu_o[:, j * size:(j + 1) * size] = small[8 + j:9 + j, :]
    for c in running[-slots:] + copies:
        c.wait()


def finish(g, small, block_out, gin, ff):
    count, feats, _ = g.shape
    micro, length, _ = block_out.shape
    sds = jax.ShapeDtypeStruct
    vec = sds((1, feats), F32)
    outs = [sds((1, micro, 1, length, feats), BF), sds((1, micro, 1, length, feats), F32), vec, vec, sds((1, feats, 3 * feats), F32), vec, vec,
            sds((1, feats, feats), F32), vec, vec, vec, sds((1, feats, ff), F32), sds((1, ff), F32), sds((1, ff, feats), F32), vec]
    return pl.pallas_call(
        finish_kernel,
        out_shape=outs,
        in_specs=[HBM] * 4,
        out_specs=[ANY if len(o.shape) > 2 else VM for o in outs],
        scratch_shapes=[pltpu.VMEM((count, feats, feats), BF), pltpu.VMEM((4, feats, feats), F32), pltpu.VMEM((16, feats), F32),
                        pltpu.VMEM(block_out.shape, BF), pltpu.VMEM(gin.shape, F32), pltpu.SemaphoreType.DMA((count,)),
                        pltpu.SemaphoreType.DMA((count,)), pltpu.SemaphoreType.DMA((5,))],
        compiler_params=pltpu.CompilerParams(vmem_limit_bytes=40 * 2**20),
        name="finish",
    )(*[pltpu.with_memory_space_constraint(v, pltpu.HBM) for v in (g, small, block_out, gin)])


def per_device(inputs, cotangent, segments, norm1_gain, norm1_shift, w_qkv, bias_query, bias_value, w_out, bias_out,
               norm2_gain, norm2_shift, w_up, bias_up, w_down, bias_down):
    weights = (w_qkv, w_out, w_up, w_down)
    vecs = (norm1_gain, norm1_shift, bias_query, bias_value, bias_out, norm2_gain, norm2_shift, bias_up, bias_down)
    block_out, gin, n1, st, mt, rl, n2, ul, hid, dl, ln = relay(segments, inputs, cotangent, weights, vecs)[:11]
    g, small = exchange(lax.axis_size("dp"), n1, st, mt, rl, n2, ul, hid, dl, ln)
    return tuple(finish(g, small, block_out, gin, w_up.shape[2]))


def solution(mesh):
    data, seg, vec, mat = P(None, "dp", None, None), P(None, "dp", None), P("section", None), P("section", None, None)
    act = P("section", None, "dp", None, None)
    in_specs = (data, data, seg, vec, vec, mat, vec, vec, mat, vec, vec, vec, mat, vec, mat, vec)
    out_specs = (act, act, vec, vec, mat, vec, vec, mat, vec, vec, vec, mat, vec, mat, vec)
    return jax.shard_map(per_device, mesh=mesh, in_specs=in_specs, out_specs=out_specs, check_vma=False)
```

profile of v0, /device:TPU:0, one launch (start us, length us, event | category | flops | bytes accessed | tf_op | source)
XLA Modules:
  0.0 323.3 jit_solution(16809649672538795995)
XLA Ops:
  0.7 151.9 %layer_relay.1 = (bf16[2,512,768]{2,1,0:T(8,128)(2,1)}, f32[2,512,768]{2,1,0:T(8,128)}, bf16[2,512,768]{2,1,0:T(8,128)(2,1)}, bf16[2,512,2304]{2,1,0:T(8,128)(2,...) custom-call(s32[2,1,512]{2,1,0:T(1,128)} %seg_ref.1, ...), custom_call_target="tpu_custom_call" | custom-call | tf_op jit(solution)/shard_map/layer_relay/pallas_call | solution.py:501
  152.6 152.9 %grad_exchange.1 = (bf16[12,768,768]{2,1,0:T(8,128)(2,1)}, f32[16,768]{1,0:T(8,128)}, bf16[16,128]{1,0:T(8,128)(2,1)}) custom-call(bf16[2,512,768]{2,1,0:T(8,128)(2,1)} %get-tuple-element.28.n1_hbm, bf16[2,512,2304]{2,1,0:T(8,128)(2,1)} %get-tuple-element.29.st_hbm, bf16[2,768,512]{2,1,0:T(8,128)(2,1)} %get-tuple-element.30.mt_hbm, ...), custom_call_target="tpu_custom_call" | custom-call | tf_op jit(solution)/shard_map/grad_exchange/pallas_call | solution.py:894
  305.5 17.7 %finish.1 = (bf16[1,2,1,512,768]{4,3,2,1,0:T(8,128)(2,1)}, f32[1,2,1,512,768]{4,3,2,1,0:T(8,128)}, f32[1,768]{1,0:T(1,128)}, f32[1,768]{1,0:T(1,128)}, f32[1,768...) custom-call(bf16[12,768,768]{2,1,0:T(8,128)(2,1)} %get-tuple-element, ...), custom_call_target="tpu_custom_call" | custom-call | tf_op jit(solution)/shard_map/finish/pallas_call | solution.py:978
where the time goes:
time: 324 us; the launch traced here: 323 us
  Pallas kernels  322 us (99%)
    pallas_call x1, Pallas kernels, exchange(): pl.pallas_call(functools.partial(exchange_kernel, group), out_shape=[sds(...  153 us
    pallas_call x1, Pallas kernels, relay(): pl.pallas_call(relay_kernel, out_shape=outs, in_specs=[VM] + [ANY] * 6 +...  152 us
    pallas_call x1, Pallas kernels, finish(): pl.pallas_call(finish_kernel, out_shape=outs, in_specs=[HBM] * 4, out_spe...  17.7 us

commit v1 on v0

--- a/solution.py
+++ b/solution.py
@@ -189,10 +189,10 @@
         outs.start("n1", n1, n1_o.at[m])
         before(("e", e_v, e_o), ("li", li, li_o), ("mt", mt, mt_o.at[0]))
 
-        @pl.loop(0, heads // GROUP)
+        @pl.loop(0, heads // heads)
         def _(group):
             def spot(i):
-                return group * GROUP + i, pl.multiple_of((group * (GROUP // 2) + i // 2) * 128, 128), i % 2
+                return group * heads + i, pl.multiple_of((group * (heads // 2) + i // 2) * 128, 128), i % 2
 
             def score(i):
                 _, at, h = spot(i)
@@ -212,12 +212,12 @@
                 li[pl.ds(head, 1), :] = inv
                 mt[pl.ds(pl.multiple_of(head * HEAD_DIM, HEAD_DIM), HEAD_DIM), :] = (ot[mine] * inv).astype(BF)
 
-            for t in range(GROUP + 2):
-                if t < GROUP:
+            for t in range(heads + 2):
+                if t < heads:
                     score(t)
                 if 0 <= t - 2:
                     mix(t - 2)
-                if 0 <= t - 1 < GROUP:
+                if 0 <= t - 1 < heads:
                     expo(t - 1)
 
         outs.start("mt", mt, mt_o.at[m])

time: 324 us -> 322 us (level)
  no operation moved by 1% of the time
where the time goes in v1:
time: 322 us
  Pallas kernels  321 us (100%)
    pallas_call x1, Pallas kernels, exchange(): pl.pallas_call(functools.partial(exchange_kernel, group), out_shape=[sds(...  153 us
    pallas_call x1, Pallas kernels, relay(): pl.pallas_call(relay_kernel, out_shape=outs, in_specs=[VM] + [ANY] * 6 +...  151 us
    pallas_call x1, Pallas kernels, finish(): pl.pallas_call(finish_kernel, out_shape=outs, in_specs=[HBM] * 4, out_spe...  17.7 us

profile of v1, /device:TPU:0, one launch (start us, length us, event | category | flops | bytes accessed | tf_op | source)
XLA Modules:
  0.0 322.0 jit_solution(11407018165186367357)
XLA Ops:
  0.7 150.6 %layer_relay.1 = (bf16[2,512,768]{2,1,0:T(8,128)(2,1)}, f32[2,512,768]{2,1,0:T(8,128)}, bf16[2,512,768]{2,1,0:T(8,128)(2,1)}, bf16[2,512,2304]{2,1,0:T(8,128)(2,...) custom-call(s32[2,1,512]{2,1,0:T(1,128)} %seg_ref.1, ...), custom_call_target="tpu_custom_call" | custom-call | tf_op jit(solution)/shard_map/layer_relay/pallas_call | solution.py:501
  151.2 152.9 %grad_exchange.1 = (bf16[12,768,768]{2,1,0:T(8,128)(2,1)}, f32[16,768]{1,0:T(8,128)}, bf16[16,128]{1,0:T(8,128)(2,1)}) custom-call(bf16[2,512,768]{2,1,0:T(8,128)(2,1)} %get-tuple-element.28.n1_hbm, bf16[2,512,2304]{2,1,0:T(8,128)(2,1)} %get-tuple-element.29.st_hbm, bf16[2,768,512]{2,1,0:T(8,128)(2,1)} %get-tuple-element.30.mt_hbm, ...), custom_call_target="tpu_custom_call" | custom-call | tf_op jit(solution)/shard_map/grad_exchange/pallas_call | solution.py:894
  304.1 17.7 %finish.1 = (bf16[1,2,1,512,768]{4,3,2,1,0:T(8,128)(2,1)}, f32[1,2,1,512,768]{4,3,2,1,0:T(8,128)}, f32[1,768]{1,0:T(1,128)}, f32[1,768]{1,0:T(1,128)}, f32[1,768...) custom-call(bf16[12,768,768]{2,1,0:T(8,128)(2,1)} %get-tuple-element, ...), custom_call_target="tpu_custom_call" | custom-call | tf_op jit(solution)/shard_map/finish/pallas_call | solution.py:978
